TPU v7x, 128 devices: a whole 4x4x4 slice. The times are simulated.
128 devices in a mesh: pipe: 4 (over y_lo, core), dp: 32 (over y_hi, z, x).
Axes of the slice: x: 4, y: 4 (y_hi: 2, y_lo: 2; y = y_hi * 2 + y_lo), z: 4, core: 2. Of those that a mesh axis runs over, the one named last changes fastest.
Arguments:
- stash: bfloat16 [4, 2, 5120, 6144], P('pipe', None, 'dp'), may hold values from -6 to 6
- attn: bfloat16 [4, 2, 32, 6, 160, 160], P('pipe', None, 'dp'), may hold values from 0 to 0.03930664
- w_value: bfloat16 [4, 6144, 768], P('pipe'), may hold values from -0.078125 to 0.078125
- w_out: bfloat16 [4, 768, 6144], P('pipe'), may hold values from -0.21875 to 0.21875
- out_grad: bfloat16 [2, 5120, 6144], P(None, 'dp', 'pipe'), may hold values from -6 to 6
- order: int32 [2], replicated, may hold values from 0 to 1, each once
- check_rows: int32 [8, 6144], replicated, may hold values from -3 to 3
Outputs:
- grad_value: float32 [4, 6144, 768], P('pipe', 'dp')
- grad_out_t: float32 [4, 6144, 768], P('pipe', 'dp')
- checksums: float32 [4, 2, 8, 768], P('pipe')
- input_grad: bfloat16 [2, 5120, 6144], P(None, 'dp', 'pipe')
Inputs may be any that keep to these rules, and one draw needn't show every extreme that they name: `order`: a permutation of the micro-batches.
All inputs are finite; a program needn't handle non-finite values.
Results may differ from a plain program's by a relative error of at most 0.022.
Values may be sent and summed in bfloat16 or wider, within the bound.
No kernel may reach another device: no remote copies, remote signals or barrier semaphores. Data moves between devices by JAX's collectives and lax.ppermute only.
A program may use at most 192 MiB of HBM per device.

v0:
```python
import jax
import jax.numpy as jnp
from jax import lax
from jax.sharding import PartitionSpec as P


def passed_along(block, axis, distance):
    devices = range(lax.axis_size(axis))
    route = [(i - distance, i) for i in devices if i - distance in devices]
    return lax.ppermute(block, axis, route)


def from_root(array, axis, root):
    mine = lax.axis_index(axis) == root
    return lax.psum(jnp.where(mine, array, jnp.zeros_like(array)), axis)


def on_device(stash, attn, w_value, w_out, out_grad, order, check_rows):
    npipe = lax.axis_size("pipe")
    section = lax.axis_index("pipe")
    inputs = stash[0]
    probs = attn[0][:, 0]
    wv = w_value[0]
    wo = w_out[0]
    micro = inputs.shape[0]
    seq = inputs.shape[1]
    width = inputs.shape[2]
    inner = wv.shape[1]
    heads = probs.shape[1]
    head_dim = inner // heads
    grad_scale = jnp.float32((micro * seq * lax.axis_size("dp")) ** (-0.5))
    check_scale = jnp.float32(width ** (-0.5))
    causal = (jnp.arange(seq)[:, None] >= jnp.arange(seq)[None, :]).astype(jnp.bfloat16)
    top_grad = lax.all_gather(out_grad, "pipe", axis=2, tiled=True)

    def backward_step(operands):
        xm, pm, dy = operands
        weights = pm * causal
        values = jnp.dot(xm, wv, preferred_element_type=jnp.float32).astype(jnp.bfloat16)
        context = jnp.einsum(
            "hij,jhd->ihd",
            weights,
            values.reshape(seq, heads, head_dim),
            preferred_element_type=jnp.float32,
        )
        context = context.reshape(seq, inner).astype(jnp.bfloat16)
        dctx = jnp.dot(dy, wo.T, preferred_element_type=jnp.float32).astype(jnp.bfloat16)
        dvals = jnp.einsum(
            "hij,ihd->jhd",
            weights,
            dctx.reshape(seq, heads, head_dim),
            preferred_element_type=jnp.float32,
        )
        dvals = dvals.reshape(seq, inner).astype(jnp.bfloat16)
        dx = (
            dy.astype(jnp.float32) + jnp.dot(dvals, wv.T, preferred_element_type=jnp.float32)
        ).astype(jnp.bfloat16)
        return (context, dvals, dx)

    def skip_step(operands):
        return (
            jnp.zeros((seq, inner), jnp.bfloat16),
            jnp.zeros((seq, inner), jnp.bfloat16),
            jnp.zeros((seq, width), jnp.bfloat16),
        )

    ctx_store = jnp.zeros((micro, seq, inner), jnp.bfloat16)
    dv_store = jnp.zeros((micro, seq, inner), jnp.bfloat16)
    dy_store = jnp.zeros((micro, seq, width), jnp.bfloat16)
    dx_store = jnp.zeros((micro, seq, width), jnp.bfloat16)
    incoming = jnp.zeros((seq, width), jnp.bfloat16)
    last_turn = micro + npipe - 2
    for turn in range(micro + npipe - 1):
        step = turn - (npipe - 1 - section)
        valid = jnp.logical_and(step >= 0, step < micro)
        slot = jnp.clip(step, 0, micro - 1)
        batch = order[slot]
        dy = jnp.where(
            section == npipe - 1, lax.dynamic_index_in_dim(top_grad, slot, 0, False), incoming
        )
        xm = lax.dynamic_index_in_dim(inputs, batch, 0, False)
        pm = lax.dynamic_index_in_dim(probs, batch, 0, False)
        context, dvals, dx = lax.cond(valid, backward_step, skip_step, (xm, pm, dy))
        ctx_store = jnp.where(
            valid, lax.dynamic_update_index_in_dim(ctx_store, context, batch, 0), ctx_store
        )
        dv_store = jnp.where(
            valid, lax.dynamic_update_index_in_dim(dv_store, dvals, batch, 0), dv_store
        )
        dy_store = jnp.where(
            valid, lax.dynamic_update_index_in_dim(dy_store, dy, batch, 0), dy_store
        )
        dx_store = jnp.where(
            valid, lax.dynamic_update_index_in_dim(dx_store, dx, slot, 0), dx_store
        )
        if turn < last_turn:
            incoming = passed_along(dx, "pipe", -1)
    x_flat = inputs.reshape(micro * seq, width)
    dv_flat = dv_store.reshape(micro * seq, inner)
    dy_flat = dy_store.reshape(micro * seq, width)
    ctx_flat = ctx_store.reshape(micro * seq, inner)
    contract = (((0,), (0,)), ((), ()))
    ck_float = check_rows.astype(jnp.float32)
    rows = width // lax.axis_size("dp")
    columns = x_flat
    grad_v = lax.psum_scatter(
        (
            lax.dot_general(columns, dv_flat, contract, preferred_element_type=jnp.float32)
            * grad_scale
        ).astype(jnp.bfloat16),
        "dp",
        scatter_dimension=0,
        tiled=True,
    ).astype(jnp.float32)
    columns = dy_flat
    grad_o = lax.psum_scatter(
        (
            lax.dot_general(columns, ctx_flat, contract, preferred_element_type=jnp.float32)
            * grad_scale
        ).astype(jnp.bfloat16),
        "dp",
        scatter_dimension=0,
        tiled=True,
    ).astype(jnp.float32)
    first_row = lax.axis_index("dp") * rows
    ck_part = lax.dynamic_slice_in_dim(ck_float, first_row, rows, 1)
    local_checks = check_scale * jnp.stack(
        [
            jnp.dot(ck_part, grad_v, precision=lax.Precision.HIGHEST),
            jnp.dot(ck_part, grad_o, precision=lax.Precision.HIGHEST),
        ]
    )
    check_sum = lax.psum(local_checks, "dp")
    first_grads = from_root(dx_store, "pipe", 0)
    share = width // npipe
    own_part = lax.dynamic_slice_in_dim(first_grads, section * share, share, 2)
    return (grad_v[None], grad_o[None], check_sum[None], own_part)


def solution(mesh):
    return jax.shard_map(
        on_device,
        mesh=mesh,
        in_specs=(
            P("pipe", None, "dp", None),
            P("pipe", None, "dp", None, None, None),
            P("pipe", None, None),
            P("pipe", None, None),
            P(None, "dp", "pipe"),
            P(),
            P(),
        ),
        out_specs=(
            P("pipe", "dp", None),
            P("pipe", "dp", None),
            P("pipe", None, None, None),
            P(None, "dp", "pipe"),
        ),
        check_vma=False,
    )
```

profile of v0, /device:TPU:16, one launch (start us, length us, event | category | flops | bytes accessed | tf_op | source)
XLA Modules:
  0.0 1039.1 jit_solution(13033466347937102646)
XLA Ops:
  11.5 44.0 %all-gather.2.cloned.1.call-done = bf16[2,160,6144]{2,1,0:T(8,128)(2,1)} async-done(((bf16[2,160,1536]{2,1,0:T(8,128)(2,1)}), bf16[2,160,6144]{2,1,0:T(8,128)(2,1)}) %all-gather.2.cloned.1.call-update) | async-done | bytes 3932176 | tf_op jit(solution)/shard_map/all_gather | solution.py:34
  57.9 4.3 select_dynamic-update-slice_fusion.5
  70.8 5.2 fusion.125
  86.4 19.1 %collective-permute-done.1 = bf16[160,6144]{1,0:T(8,128)(2,1)S(1)} collective-permute-done((bf16[160,6144]{1,0:T(8,128)(2,1)}, bf16[160,6144]{1,0:T(8,128)(2,1)S(1)}, u32[]{:S(2)}, u32[]{:S(2)}) %collective-permute-start.1) | collective-permute-done | bytes 1966112 | tf_op jit(solution)/shard_map/ppermute | solution.py:10
  106.8 5.4 fusion.124
  112.9 4.6 conditional.7
  127.0 53.4 %collective-permute-done.2 = bf16[160,6144]{1,0:T(8,128)(2,1)S(1)} collective-permute-done((bf16[160,6144]{1,0:T(8,128)(2,1)}, bf16[160,6144]{1,0:T(8,128)(2,1)S(1)}, u32[]{:S(2)}, u32[]{:S(2)}) %collective-permute-start.2) | collective-permute-done | bytes 1966112 | tf_op jit(solution)/shard_map/ppermute | solution.py:10
  180.4 4.1 fusion.123
  184.6 21.8 %conditional.8 = (bf16[160,6144]{1,0:T(8,128)(2,1)}, bf16[1,160,768]{2,1,0:T(8,128)(2,1)}, bf16[1,160,768]{2,1,0:T(8,128)(2,1)S(1)}, bf16[1,160,6144]{2,1,0:T(8,128)(2,1)}) conditional(s32[]{:T(128)} %convert_element_type.329, () %tuple.104, (bf16[160,6144]{1,0:T(8,128)(2,1)S(1)}, bf16[768,6144]{1,0:T(8,128)(2,1)S(1)}, ...), branch_computations={%region_6.7_spmd, %region_7.8_spmd} | conditional | flops 4612700160 | bytes 89258160 | solution.py:83
  191.3 8.3 fusion.73
  211.2 4.2 select_dynamic-update-slice_fusion.1
  215.4 17.1 %collective-permute-done.3 = bf16[160,6144]{1,0:T(8,128)(2,1)S(1)} collective-permute-done((bf16[160,6144]{1,0:T(8,128)(2,1)}, bf16[160,6144]{1,0:T(8,128)(2,1)S(1)}, u32[]{:S(2)}, u32[]{:S(2)}) %collective-permute-start.3) | collective-permute-done | bytes 1966112 | tf_op jit(solution)/shard_map/ppermute | solution.py:10
  236.6 18.0 %conditional.9 = (bf16[1,160,768]{2,1,0:T(8,128)(2,1)}, bf16[1,160,768]{2,1,0:T(8,128)(2,1)}, bf16[1,160,6144]{2,1,0:T(8,128)(2,1)}) conditional(s32[]{:T(128)} %convert_element_type.330, () %tuple.106, (bf16[1,2,160,6144]{3,2,1,0:T(8,128)(2,1)}, s32[]{:T(128)}, bf16[6144,768]{1,0:T(8,128)(2,1)}, bf16[1,2,1,6,160,160]{5,4,3,2,1,0:T(8,128)(2,1)S(1)}, ...), branch_computations={%region_8.9_spmd, %region_9.10_spmd} | conditional | flops 4612700160 | bytes 98173048 | solution.py:83
  238.2 7.1 fusion.105
  245.6 4.6 fusion.97
  254.6 4.1 select_dynamic-update-slice_fusion
  258.7 4.2 broadcast_select_fusion
  266.4 9.6 fusion.120
  278.1 9.6 fusion.121
  287.7 12.7 %copy.109 = bf16[6144,768]{1,0:T(8,128)(2,1)} copy(bf16[6144,768]{0,1:T(8,128)(2,1)} %fusion.121) | data formatting | bytes 18874368
  300.4 53.4 %all-reduce.2.cloned.1.call-done = bf16[2,160,6144]{2,1,0:T(8,128)(2,1)} async-done(((bf16[2,160,6144]{2,1,0:T(8,128)(2,1)}), bf16[2,160,6144]{2,1,0:T(8,128)(2,1)}) %all-reduce.2.cloned.1.call-update) | async-done | bytes 3932176 | tf_op jit(solution)/shard_map/psum | solution.py:15
  356.1 245.0 %reduce-scatter.5.cloned.1.call-done = bf16[192,768]{1,0:T(8,128)(2,1)} async-done(((bf16[6144,768]{1,0:T(8,128)(2,1)}), bf16[192,768]{1,0:T(8,128)(2,1)}) %reduce-scatter.5.cloned.1.call-update) | async-done | bytes 294928 | tf_op jit(solution)/shard_map/reduce_scatter | solution.py:116
  602.3 243.8 %reduce-scatter.7.cloned.1.call-done = bf16[192,768]{1,0:T(8,128)(2,1)} async-done(((bf16[6144,768]{1,0:T(8,128)(2,1)}), bf16[192,768]{1,0:T(8,128)(2,1)}) %reduce-scatter.7.cloned.1.call-update) | async-done | bytes 294928
  847.4 181.8 %psum.14 = f32[1,2,8,768]{3,2,1,0:T(8,128)} all-reduce(f32[1,2,8,768]{3,2,1,0:T(8,128)S(1)} %fusion.127), channel_id=1, replica_groups=mesh['pipe'=4,'dp'=32] {'dp'}, use_global_device_ids=true, to_apply=%region_12.13 | all-reduce | flops 12288 | bytes 98304 | tf_op jit(solution)/shard_map/psum | solution.py:133
  (131 shorter events, 78.1 us)
Async XLA Ops:
  7.2 48.3 %all-gather.2.cloned.1.call-start = ((), (), s32[]{:S(2)}) async-start(), calls=%async_computation.2 | async-start | bytes 4915200 | tf_op jit(solution)/shard_map/all_gather | solution.py:34
  7.9 346.0 %all-reduce.2.cloned.1.call-start = ((), (), s32[]{:S(2)}) async-start(), calls=%async_computation.4 | async-start | bytes 7864320 | tf_op jit(solution)/shard_map/psum | solution.py:15
  55.5 7.0 copy-start.1
  64.3 6.5 copy-start.6
  64.3 11.7 %copy-start.20 = (bf16[1,160,768]{2,1,0:T(8,128)(2,1)}, bf16[1,160,768]{2,1,0:T(8,128)(2,1)S(1)}, u32[]{:S(2)}) copy-start(bf16[1,160,768]{2,1,0:T(8,128)(2,1)S(1)} %get-tuple-element.362) | copy-start | bytes 737284
  64.4 11.7 %copy-start.22 = (bf16[1,160,768]{2,1,0:T(8,128)(2,1)}, bf16[1,160,768]{2,1,0:T(8,128)(2,1)S(1)}, u32[]{:S(2)}) copy-start(bf16[1,160,768]{2,1,0:T(8,128)(2,1)S(1)} %get-tuple-element.353) | copy-start | bytes 737284
  64.4 6.5 collective-permute-start
  79.3 33.6 %copy-start.17 = (bf16[1,160,768]{2,1,0:T(8,128)(2,1)}, bf16[1,160,768]{2,1,0:T(8,128)(2,1)S(1)}, u32[]{:S(2)}) copy-start(bf16[1,160,768]{2,1,0:T(8,128)(2,1)S(1)} %get-tuple-element.355) | copy-start | bytes 737284
  79.3 26.1 %collective-permute-start.1 = (bf16[160,6144]{1,0:T(8,128)(2,1)}, bf16[160,6144]{1,0:T(8,128)(2,1)S(1)}, u32[]{:S(2)}, u32[]{:S(2)}) collective-permute-start(bf16[160,6144]{1,0:T(8,128)(2,1)} %get-tuple-element.356), channel_id=1, source_target_pairs={{32,0},{64,32},{96,64},{33,1},{65,33},{97,65},{34,2},{66,34},{98,6... | collective-permute-start | bytes 5898248 | tf_op jit(solution)/shard_map/ppermute | solution.py:10
  117.6 62.9 %collective-permute-start.2 = (bf16[160,6144]{1,0:T(8,128)(2,1)}, bf16[160,6144]{1,0:T(8,128)(2,1)S(1)}, u32[]{:S(2)}, u32[]{:S(2)}) collective-permute-start(bf16[160,6144]{1,0:T(8,128)(2,1)} %get-tuple-element.358), channel_id=1, source_target_pairs={{32,0},{64,32},{96,64},{33,1},{65,33},{97,65},{34,2},{66,34},{98,6... | collective-permute-start | bytes 5898248 | tf_op jit(solution)/shard_map/ppermute | solution.py:10
  121.4 63.2 %slice-start.12 = ((s8[9437184]{0:T(1024)(128)(4,1)}), s8[4194304]{0:T(1024)(128)(4,1)S(1)}, s32[]{:S(2)}) async-start(s8[9437184]{0:T(1024)(128)(4,1)} %bitcast.268), calls=%async_computation.18 | async-start | bytes 8388608
  123.1 57.3 %copy-start.3 = (bf16[2,160,6144]{2,1,0:T(8,128)(2,1)S(1)}, bf16[2,160,6144]{2,1,0:T(8,128)(2,1)}, u32[]{:S(2)}) copy-start(bf16[2,160,6144]{2,1,0:T(8,128)(2,1)} %all-gather.2.cloned.1.call-done) | copy-start | bytes 11796484
  123.1 61.5 %slice-start.13 = ((s8[9437184]{0:T(1024)(128)(4,1)}), s8[4194304]{0:T(1024)(128)(4,1)S(1)}, s32[]{:S(2)}) async-start(s8[9437184]{0:T(1024)(128)(4,1)} %bitcast.268), calls=%async_computation.19 | async-start | bytes 8388608
  189.7 13.1 %slice-start.9 = ((s8[9437184]{0:T(1024)(128)(4,1)}), s8[4194304]{0:T(1024)(128)(4,1)S(1)}, s32[]{:S(2)}) async-start(s8[9437184]{0:T(1024)(128)(4,1)} %bitcast.262), calls=%async_computation.15 | async-start | bytes 8388608 | tf_op jit(solution)/shard_map/cond
  191.2 11.5 %slice-start.10 = ((s8[9437184]{0:T(1024)(128)(4,1)}), s8[4194304]{0:T(1024)(128)(4,1)S(1)}, s32[]{:S(2)}) async-start(s8[9437184]{0:T(1024)(128)(4,1)} %bitcast.262), calls=%async_computation.16 | async-start | bytes 8388608 | tf_op jit(solution)/shard_map/cond
  191.3 11.5 %slice-start.11 = ((s8[9437184]{0:T(1024)(128)(4,1)}), s8[1048576]{0:T(1024)(128)(4,1)S(1)}, s32[]{:S(2)}) async-start(s8[9437184]{0:T(1024)(128)(4,1)} %bitcast.262), calls=%async_computation.17 | async-start | bytes 2097152 | tf_op jit(solution)/shard_map/cond
  206.4 9.0 copy-start.24
  206.4 26.1 %collective-permute-start.3 = (bf16[160,6144]{1,0:T(8,128)(2,1)}, bf16[160,6144]{1,0:T(8,128)(2,1)S(1)}, u32[]{:S(2)}, u32[]{:S(2)}) collective-permute-start(bf16[160,6144]{1,0:T(8,128)(2,1)} %get-tuple-element.360), channel_id=1, source_target_pairs={{32,0},{64,32},{96,64},{33,1},{65,33},{97,65},{34,2},{66,34},{98,6... | collective-permute-start | bytes 5898248 | tf_op jit(solution)/shard_map/ppermute | solution.py:10
  211.2 21.4 %copy-start.4 = (bf16[2,160,6144]{2,1,0:T(8,128)(2,1)S(1)}, bf16[2,160,6144]{2,1,0:T(8,128)(2,1)}, u32[]{:S(2)}) copy-start(bf16[2,160,6144]{2,1,0:T(8,128)(2,1)} %all-gather.2.cloned.1.call-done) | copy-start | bytes 11796484
  238.2 7.1 copy-start.13
  238.2 7.4 copy-start
  263.0 338.1 %reduce-scatter.5.cloned.1.call-start = ((), (), s32[]{:S(2)}) async-start(), calls=%async_computation.3 | async-start | bytes 9732096 | tf_op jit(solution)/shard_map/reduce_scatter | solution.py:116
  276.1 570.1 %reduce-scatter.7.cloned.1.call-start = ((), (), s32[]{:S(2)}) async-start(), calls=%async_computation.5 | async-start | bytes 9732096
  601.0 430.5 %copy-start.16 = (bf16[192,768]{1,0:T(8,128)(2,1)S(1)}, bf16[192,768]{1,0:T(8,128)(2,1)}, u32[]{:S(2)}) copy-start(bf16[192,768]{1,0:T(8,128)(2,1)} %reduce-scatter.5.cloned.1.call-done) | copy-start | bytes 884740
  (12 other events, 33.8 us)
Sparse Core Ops, SparseCore 0:
  9.7 45.7 all-gather.1
  263.1 90.7 all-reduce.1
  359.2 241.7 reduce-scatter.4
  606.2 239.8 reduce-scatter.6
where the time goes:
time: 1050 us; the launch traced here: 1040 us
  waiting for transfers between devices  680 us (65%)
  blocking collectives  182 us (17%)
  matrix products  51.8 us (5%)
  other arithmetic  49.2 us (5%)
  local copies, waits for them, and re-layouts  45.9 us (4%)
  between operations  23.8 us (2%)
    reduce_scatter x1, waiting for transfers between devices, on_device(): lax.psum_scatter((lax.dot_general(columns, ctx_flat, contract, preferred_...  245 us
    unnamed x5, waiting for transfers between devices  245 us
    psum x1, blocking collectives, on_device(): check_sum = lax.psum(local_checks, 'dp')  182 us
    ppermute x4, waiting for transfers between devices, passed_along(): return lax.ppermute(block, axis, route)  93 us
    psum x1, waiting for transfers between devices, from_root(): return lax.psum(jnp.where(mine, array, jnp.zeros_like(array)), axis)  53.4 us
    all_gather x1, waiting for transfers between devices, on_device(): top_grad = lax.all_gather(out_grad, 'pipe', axis=2, tiled=True)  44 us
    select_n x5, other arithmetic, on_device(): jnp.where(valid, lax.dynamic_update_index_in_dim(dy_store, dy, batch, 0),...  23 us
  transfers between devices with their start and end apart: 8, of which 8 were waited for; matrix products, arithmetic and copies ran while one was open for 5% of the time, Pallas kernels for 0%

commit v1 on v0

--- a/solution.py
+++ b/solution.py
@@ -130,7 +130,7 @@
             jnp.dot(ck_part, grad_o, precision=lax.Precision.HIGHEST),
         ]
     )
-    check_sum = lax.psum(local_checks, "dp")
+    check_sum = lax.all_gather(local_checks, "dp").sum(axis=0)
     first_grads = from_root(dx_store, "pipe", 0)
     share = width // npipe
     own_part = lax.dynamic_slice_in_dim(first_grads, section * share, share, 2)

time: 1050 us -> 945 us (0.900)
  blocking collectives: 182 us -> 0 us
  waiting for transfers between devices: 680 us -> 760 us
    psum x1 -> x0, blocking collectives: 182 us -> none  [on_device(): check_sum = lax.psum(local_checks, 'dp')]
    all_gather x0 -> x1, waiting for transfers between devices: none -> 65.5 us  [on_device(): check_sum = lax.all_gather(local_checks, 'dp').sum(axis=0)]
    psum x1, waiting for transfers between devices: 53.4 us -> 86.6 us  [from_root(): return lax.psum(jnp.where(mine, array, jnp.zeros_like(array)), axis)]
    reduce_scatter x1, waiting for transfers between devices: 245 us -> 213 us  [on_device(): lax.psum_scatter((lax.dot_general(columns, ctx_flat, contract, preferred_...]
    ppermute x4, waiting for transfers between devices: 93 us -> 106 us  [passed_along(): return lax.ppermute(block, axis, route)]
    select_n x5, other arithmetic: 17.4 us -> 6.56 us  [on_device(): jnp.where(valid, lax.dynamic_update_index_in_dim(dx_store, dx, slot, 0),...]
    unnamed x43 -> x37, local copies, waits for them, and re-layouts: 18.5 us -> 21.3 us
    unnamed x5 -> x6, waiting for transfers between devices: 245 us -> 245 us
  transfers between devices with their start and end apart: 8 -> 9, of which waited for: 8 -> 9; matrix products, arithmetic and copies ran while one was open for 5% -> 5% of each run, Pallas kernels for 0% -> 0%
where the time goes in v1:
time: 945 us; the launch traced here: 933 us
  waiting for transfers between devices  760 us (80%)
  matrix products  54.1 us (6%)
  local copies, waits for them, and re-layouts  47.3 us (5%)
  other arithmetic  40.7 us (4%)
  between operations  24.5 us (3%)
    unnamed x6, waiting for transfers between devices  245 us
    reduce_scatter x1, waiting for transfers between devices, on_device(): lax.psum_scatter((lax.dot_general(columns, ctx_flat, contract, preferred_...  213 us
    ppermute x4, waiting for transfers between devices, passed_along(): return lax.ppermute(block, axis, route)  106 us
    psum x1, waiting for transfers between devices, from_root(): return lax.psum(jnp.where(mine, array, jnp.zeros_like(array)), axis)  86.6 us
    all_gather x1, waiting for transfers between devices, on_device(): check_sum = lax.all_gather(local_checks, 'dp').sum(axis=0)  65.5 us
    all_gather x1, waiting for transfers between devices, on_device(): top_grad = lax.all_gather(out_grad, 'pipe', axis=2, tiled=True)  44 us
    select_n x5, other arithmetic, on_device(): jnp.where(valid, lax.dynamic_update_index_in_dim(dy_store, dy, batch, 0),...  24.8 us
    unnamed x37, local copies, waits for them, and re-layouts  21.3 us
  transfers between devices with their start and end apart: 9, of which 9 were waited for; matrix products, arithmetic and copies ran while one was open for 5% of the time, Pallas kernels for 0%

profile of v1, /device:TPU:16, one launch (start us, length us, event | category | flops | bytes accessed | tf_op | source)
XLA Modules:
  0.0 933.5 jit_solution(16920493250119993928)
XLA Ops:
  11.5 44.0 %all-gather.3.cloned.1.call-done = bf16[2,160,6144]{2,1,0:T(8,128)(2,1)} async-done(((bf16[2,160,1536]{2,1,0:T(8,128)(2,1)}), bf16[2,160,6144]{2,1,0:T(8,128)(2,1)}) %all-gather.3.cloned.1.call-update) | async-done | bytes 3932176 | tf_op jit(solution)/shard_map/all_gather | solution.py:34
  57.9 4.3 select_dynamic-update-slice_fusion.5
  72.2 5.2 fusion.125
  77.4 3.2 conditional.6
  84.1 22.7 %collective-permute-done.1 = bf16[160,6144]{1,0:T(8,128)(2,1)S(1)} collective-permute-done((bf16[160,6144]{1,0:T(8,128)(2,1)}, bf16[160,6144]{1,0:T(8,128)(2,1)S(1)}, u32[]{:S(2)}, u32[]{:S(2)}) %collective-permute-start.1) | collective-permute-done | bytes 1966112 | tf_op jit(solution)/shard_map/ppermute | solution.py:10
  108.1 5.4 fusion.124
  114.3 4.8 conditional.7
  122.3 58.6 %collective-permute-done.2 = bf16[160,6144]{1,0:T(8,128)(2,1)S(1)} collective-permute-done((bf16[160,6144]{1,0:T(8,128)(2,1)}, bf16[160,6144]{1,0:T(8,128)(2,1)S(1)}, u32[]{:S(2)}, u32[]{:S(2)}) %collective-permute-start.2) | collective-permute-done | bytes 1966112 | tf_op jit(solution)/shard_map/ppermute | solution.py:10
  182.2 5.2 fusion.123
  187.4 23.8 %conditional.8 = (bf16[160,6144]{1,0:T(8,128)(2,1)}, bf16[1,160,768]{2,1,0:T(8,128)(2,1)S(1)}, bf16[1,160,768]{2,1,0:T(8,128)(2,1)S(1)}, bf16[1,160,6144]{2,1,0:T(8,128)(2,1)}) conditional(s32[]{:T(128)} %convert_element_type.329, () %tuple.104, (bf16[160,6144]{1,0:T(8,128)(2,1)S(1)}, bf16[768,6144]{1,0:T(8,128)(2,1)}, ...), branch_computations={%region_6.7_spmd, %region_7.8_spmd} | conditional | flops 4612700160 | bytes 89258160 | solution.py:83
  187.6 6.9 fusion.81
  196.7 8.4 fusion.73
  215.7 21.7 %collective-permute-done.3 = bf16[160,6144]{1,0:T(8,128)(2,1)S(1)} collective-permute-done((bf16[160,6144]{1,0:T(8,128)(2,1)}, bf16[160,6144]{1,0:T(8,128)(2,1)S(1)}, u32[]{:S(2)}, u32[]{:S(2)}) %collective-permute-start.3) | collective-permute-done | bytes 1966112 | tf_op jit(solution)/shard_map/ppermute | solution.py:10
  238.7 4.6 fusion.122
  243.3 18.0 %conditional.9 = (bf16[1,160,768]{2,1,0:T(8,128)(2,1)}, bf16[1,160,768]{2,1,0:T(8,128)(2,1)}, bf16[1,160,6144]{2,1,0:T(8,128)(2,1)}) conditional(s32[]{:T(128)} %convert_element_type.330, () %tuple.106, (bf16[1,2,160,6144]{3,2,1,0:T(8,128)(2,1)}, s32[]{:T(128)}, bf16[6144,768]{1,0:T(8,128)(2,1)}, bf16[1,2,1,6,160,160]{5,4,3,2,1,0:T(8,128)(2,1)S(1)}, ...), branch_computations={%region_8.9_spmd, %region_9.10_spmd} | conditional | flops 4612700160 | bytes 100139184 | solution.py:83
  244.9 7.1 fusion.105
  252.3 4.5 fusion.97
  263.1 9.1 fusion.120
  274.2 9.6 %fusion.121 = bf16[6144,768]{0,1:T(8,128)(2,1)} fusion(bf16[320,768]{1,0:T(8,128)(2,1)S(1)} %bitcast.268, bf16[320,6144]{1,0:T(8,128)(2,1)} %bitcast.269), kind=kOutput, calls=%fused_computation.128 | convolution fusion | flops 3029336064 | bytes 13860864 | tf_op jit(solution)/shard_map/dot_general | solution.py:108
  283.8 12.2 %copy.109 = bf16[6144,768]{1,0:T(8,128)(2,1)} copy(bf16[6144,768]{0,1:T(8,128)(2,1)} %fusion.121) | data formatting | bytes 18874368
  306.5 213.1 %reduce-scatter.5.cloned.1.call-done = bf16[192,768]{1,0:T(8,128)(2,1)} async-done(((bf16[6144,768]{1,0:T(8,128)(2,1)}), bf16[192,768]{1,0:T(8,128)(2,1)}) %reduce-scatter.5.cloned.1.call-update) | async-done | bytes 294928 | tf_op jit(solution)/shard_map/reduce_scatter | solution.py:116
  520.9 244.0 %reduce-scatter.7.cloned.1.call-done = bf16[192,768]{1,0:T(8,128)(2,1)} async-done(((bf16[6144,768]{1,0:T(8,128)(2,1)}), bf16[192,768]{1,0:T(8,128)(2,1)}) %reduce-scatter.7.cloned.1.call-update) | async-done | bytes 294928
  766.9 86.6 %all-reduce.2.cloned.1.call-done = bf16[2,160,6144]{2,1,0:T(8,128)(2,1)} async-done(((bf16[2,160,6144]{2,1,0:T(8,128)(2,1)}), bf16[2,160,6144]{2,1,0:T(8,128)(2,1)}) %all-reduce.2.cloned.1.call-update) | async-done | bytes 3932176 | tf_op jit(solution)/shard_map/psum | solution.py:15
  858.8 65.5 %all-gather.5.cloned.1.call-done = f32[32,2,8,768]{3,2,1,0:T(8,128)} async-done(((f32[1,2,8,768]{3,2,1,0:T(8,128)}), f32[32,2,8,768]{3,2,1,0:T(8,128)}) %all-gather.5.cloned.1.call-update) | async-done | bytes 1572880 | tf_op jit(solution)/shard_map/all_gather | solution.py:133
  (131 shorter events, 72.2 us)
Async XLA Ops:
  7.2 48.3 %all-gather.3.cloned.1.call-start = ((), (), s32[]{:S(2)}) async-start(), calls=%async_computation.2 | async-start | bytes 4915200 | tf_op jit(solution)/shard_map/all_gather | solution.py:34
  7.9 511.7 %reduce-scatter.5.cloned.1.call-start = ((), (), s32[]{:S(2)}) async-start(), calls=%async_computation.3 | async-start | bytes 9732096 | tf_op jit(solution)/shard_map/reduce_scatter | solution.py:116
  55.5 7.0 copy-start.1
  57.9 4.6 copy-start.4
  65.7 6.5 copy-start.5
  65.7 6.4 collective-permute-start
  80.6 33.6 %copy-start.21 = (bf16[1,160,768]{2,1,0:T(8,128)(2,1)}, bf16[1,160,768]{2,1,0:T(8,128)(2,1)S(1)}, u32[]{:S(2)}) copy-start(bf16[1,160,768]{2,1,0:T(8,128)(2,1)S(1)} %get-tuple-element.363) | copy-start | bytes 737284
  80.7 33.6 %copy-start.22 = (bf16[1,160,768]{2,1,0:T(8,128)(2,1)}, bf16[1,160,768]{2,1,0:T(8,128)(2,1)S(1)}, u32[]{:S(2)}) copy-start(bf16[1,160,768]{2,1,0:T(8,128)(2,1)S(1)} %get-tuple-element.355) | copy-start | bytes 737284
  80.7 26.1 %collective-permute-start.1 = (bf16[160,6144]{1,0:T(8,128)(2,1)}, bf16[160,6144]{1,0:T(8,128)(2,1)S(1)}, u32[]{:S(2)}, u32[]{:S(2)}) collective-permute-start(bf16[160,6144]{1,0:T(8,128)(2,1)} %get-tuple-element.356), channel_id=1, source_target_pairs={{32,0},{64,32},{96,64},{33,1},{65,33},{97,65},{34,2},{66,34},{98,6... | collective-permute-start | bytes 5898248 | tf_op jit(solution)/shard_map/ppermute | solution.py:10
  108.1 6.1 copy-start.2
  119.1 61.8 %collective-permute-start.2 = (bf16[160,6144]{1,0:T(8,128)(2,1)}, bf16[160,6144]{1,0:T(8,128)(2,1)S(1)}, u32[]{:S(2)}, u32[]{:S(2)}) collective-permute-start(bf16[160,6144]{1,0:T(8,128)(2,1)} %get-tuple-element.358), channel_id=1, source_target_pairs={{32,0},{64,32},{96,64},{33,1},{65,33},{97,65},{34,2},{66,34},{98,6... | collective-permute-start | bytes 5898248 | tf_op jit(solution)/shard_map/ppermute | solution.py:10
  195.3 13.0 %slice-start.9 = ((s8[9437184]{0:T(1024)(128)(4,1)}), s8[4194304]{0:T(1024)(128)(4,1)S(1)}, s32[]{:S(2)}) async-start(s8[9437184]{0:T(1024)(128)(4,1)} %bitcast.261), calls=%async_computation.16 | async-start | bytes 8388608 | tf_op jit(solution)/shard_map/cond
  196.7 11.6 %slice-start.10 = ((s8[9437184]{0:T(1024)(128)(4,1)}), s8[4194304]{0:T(1024)(128)(4,1)S(1)}, s32[]{:S(2)}) async-start(s8[9437184]{0:T(1024)(128)(4,1)} %bitcast.261), calls=%async_computation.17 | async-start | bytes 8388608 | tf_op jit(solution)/shard_map/cond
  196.7 11.6 %slice-start.11 = ((s8[9437184]{0:T(1024)(128)(4,1)}), s8[1048576]{0:T(1024)(128)(4,1)S(1)}, s32[]{:S(2)}) async-start(s8[9437184]{0:T(1024)(128)(4,1)} %bitcast.261), calls=%async_computation.18 | async-start | bytes 2097152 | tf_op jit(solution)/shard_map/cond
  211.2 26.1 %collective-permute-start.3 = (bf16[160,6144]{1,0:T(8,128)(2,1)}, bf16[160,6144]{1,0:T(8,128)(2,1)S(1)}, u32[]{:S(2)}, u32[]{:S(2)}) collective-permute-start(bf16[160,6144]{1,0:T(8,128)(2,1)} %get-tuple-element.360), channel_id=1, source_target_pairs={{32,0},{64,32},{96,64},{33,1},{65,33},{97,65},{34,2},{66,34},{98,6... | collective-permute-start | bytes 5898248 | tf_op jit(solution)/shard_map/ppermute | solution.py:10
  214.5 24.2 %copy-start.3 = (bf16[2,160,6144]{2,1,0:T(8,128)(2,1)S(1)}, bf16[2,160,6144]{2,1,0:T(8,128)(2,1)}, u32[]{:S(2)}) copy-start(bf16[2,160,6144]{2,1,0:T(8,128)(2,1)} %all-gather.3.cloned.1.call-done) | copy-start | bytes 11796484
  215.7 21.7 %copy-start.7 = (bf16[2,160,768]{2,1,0:T(8,128)(2,1)}, bf16[2,160,768]{2,1,0:T(8,128)(2,1)S(1)}, u32[]{:S(2)}) copy-start(bf16[2,160,768]{2,1,0:T(8,128)(2,1)S(1)} %select_dynamic-update-slice_fusion.7) | copy-start | bytes 1474564
  244.9 7.1 copy-start.13
  244.9 7.4 copy-start
  252.3 4.5 copy-start.18
  272.2 492.7 %reduce-scatter.7.cloned.1.call-start = ((), (), s32[]{:S(2)}) async-start(), calls=%async_computation.6 | async-start | bytes 9732096
  296.1 557.4 %all-reduce.2.cloned.1.call-start = ((), (), s32[]{:S(2)}) async-start(), calls=%async_computation.5 | async-start | bytes 7864320 | tf_op jit(solution)/shard_map/psum | solution.py:15
  306.5 617.9 %all-gather.5.cloned.1.call-start = ((), (), s32[]{:S(2)}) async-start(), calls=%async_computation.4 | async-start | bytes 1622016 | tf_op jit(solution)/shard_map/all_gather | solution.py:133
  519.6 338.4 %copy-start.20 = (bf16[192,768]{1,0:T(8,128)(2,1)S(1)}, bf16[192,768]{1,0:T(8,128)(2,1)}, u32[]{:S(2)}) copy-start(bf16[192,768]{1,0:T(8,128)(2,1)} %reduce-scatter.5.cloned.1.call-done) | copy-start | bytes 884740
  (12 other events, 26.9 us)
Sparse Core Ops, SparseCore 0:
  9.7 45.7 all-gather.2
  272.4 247.1 reduce-scatter.4
  525.0 239.9 reduce-scatter.6
  767.3 86.1 all-reduce.1
  857.0 67.3 all-gather.4
